TPU v7x, 32 devices: a whole 2x2x4 slice. The times are simulated.
32 devices in a mesh: ctx: 8 (over z, x), head: 4 (over y, core).
Axes of the slice: x: 2, y: 2, z: 4, core: 2. Of those that a mesh axis runs over, the one named last changes fastest.
Arguments:
- queries: bfloat16 [2048, 4096], P('ctx', 'head')
- keys: bfloat16 [2048, 1024], P('ctx', 'head')
- values: bfloat16 [2048, 1024], P('ctx', 'head'), may hold values from -6 to 6
- lengths: int32 [8], replicated, may hold values from 1 to 1024, 2048 in all
- out_weight: bfloat16 [4096, 4096], P('head'), may hold values from -0.375 to 0.375
Outputs:
- projected: bfloat16 [2048, 4096], P(('ctx', 'head'))
Inputs may be any that keep to these rules, and one draw needn't show every extreme that they name: The lengths sum to 2048; the longest document has exactly 1024 tokens.
All inputs are finite; a program needn't handle non-finite values.
Results may differ from a plain program's by a relative error of at most 0.015.
Values may be sent and summed in bfloat16 or wider, within the bound.
A program may use at most 64 MiB of HBM per device.

v0:
```python
import jax
import jax.numpy as jnp
from jax import lax
from jax.sharding import PartitionSpec as P

HEAD_SIZE = 128


def shifted(value, axis, steps):
    count = lax.axis_size(axis)
    first, last = (max(0, -steps), min(count, count - steps))
    return lax.ppermute(value, axis, [(source, source + steps) for source in range(first, last)])


def doc_of(positions, ends):
    return jnp.sum((positions[:, None] >= ends[None, :]).astype(jnp.int32), axis=1)


def shards(queries, keys, values, lengths, out_weight):
    tok = queries.shape[0]
    local_kv = keys.shape[1] // HEAD_SIZE
    query_group = queries.shape[1] // keys.shape[1]
    span = min(16, lax.axis_size("ctx") // 2)
    stretch = lax.axis_index("ctx")
    ends = jnp.cumsum(lengths)
    paired = jnp.stack([keys, values])
    window = paired
    have = 1
    while have < span + 1:
        count = min(have, span + 1 - have)
        received = shifted(window[:, window.shape[1] - count * tok :], "ctx", have)
        window = jnp.concatenate([received, window], axis=1)
        have = have + count
    blocks = jnp.swapaxes(window.reshape(2, span + 1, tok, local_kv * HEAD_SIZE), 0, 1)
    key_pos = (stretch - span) * tok + jnp.arange((span + 1) * tok, dtype=jnp.int32)
    key_pos = key_pos.reshape(span + 1, tok)
    query_pos = stretch * tok + jnp.arange(tok, dtype=jnp.int32)
    query_doc = doc_of(query_pos, ends)
    query_head_rows = queries.reshape(tok, local_kv, query_group, HEAD_SIZE)
    score_scale = 1.0 / HEAD_SIZE**0.5

    def step(carry, item):
        kv_block, positions = item
        allowed = (
            (doc_of(positions, ends)[None, :] == query_doc[:, None])
            & (positions[None, :] <= query_pos[:, None])
            & (positions[None, :] >= 0)
        )
        running, total, accum = carry
        key_head_rows = kv_block[0].reshape(tok, local_kv, HEAD_SIZE)
        value_heads = kv_block[1].reshape(tok, local_kv, HEAD_SIZE)
        logit_scores = (
            jnp.einsum(
                "hqnp,zqp->qnhz", query_head_rows, key_head_rows, preferred_element_type=jnp.float32
            )
            * score_scale
        )
        logit_scores = jnp.where(allowed, logit_scores, jnp.float32(-1e30))
        newest = jnp.maximum(running, jnp.max(logit_scores, axis=-1))
        factor = jnp.exp(running - newest)
        weights = jnp.where(allowed, jnp.exp(logit_scores - newest[..., None]), jnp.float32(0.0))
        total = total * factor + jnp.sum(weights, axis=-1)
        accum = accum * factor[..., None] + jnp.einsum(
            "wcju,uwn->wcjn",
            weights.astype(jnp.bfloat16),
            value_heads,
            preferred_element_type=jnp.float32,
        )
        result = (newest, total, accum)
        return (result, None)

    start_state = (
        jnp.full((local_kv, query_group, tok), -1e30, jnp.float32),
        jnp.zeros((local_kv, query_group, tok), jnp.float32),
        jnp.zeros((local_kv, query_group, tok, HEAD_SIZE), jnp.float32),
    )
    final_state, unused = lax.scan(step, start_state, (blocks, key_pos))
    attended = final_state[2] / final_state[1][..., None]
    attended = (
        jnp.transpose(attended, (2, 0, 1, 3))
        .reshape(tok, local_kv * query_group * HEAD_SIZE)
        .astype(jnp.bfloat16)
    )
    return lax.psum_scatter(
        jnp.dot(attended, out_weight, preferred_element_type=jnp.float32).astype(jnp.bfloat16),
        "head",
        scatter_dimension=0,
        tiled=True,
    )


def solution(mesh):
    in_specs = (P("ctx", "head"), P("ctx", "head"), P("ctx", "head"), P(), P("head", None))
    out_specs = P(("ctx", "head"), None)
    return jax.shard_map(shards, mesh=mesh, in_specs=in_specs, out_specs=out_specs, check_vma=False)
```

profile of v0, /device:TPU:17, one launch (start us, length us, event | category | flops | bytes accessed | tf_op | source)
XLA Modules:
  0.0 108.3 jit_solution(4448508220680306712)
XLA Ops:
  6.5 0.0 copy-start
  6.5 0.0 copy-start.1
  6.5 0.0 reduce-scatter.2.cloned.1.call-start
  6.5 1.7 %pad_maximum_fusion = bf16[2,256,256]{2,1,0:T(8,128)(2,1)} fusion(bf16[1,256,256]{2,1,0:T(8,128)(2,1)} %bitcast.61, bf16[1,256,256]{2,1,0:T(8,128)(2,1)} %bitcast.64), kind=kLoop, calls=%fused_computation.31 | loop fusion | flops 131072 | bytes 524288 | tf_op jit(solution)/shard_map/stack | solution.py:26
  8.3 3.1 %collective-permute-start.1 = (bf16[2,256,256]{2,1,0:T(8,128)(2,1)}, bf16[2,256,256]{2,1,0:T(8,128)(2,1)S(1)}, u32[]{:S(2)}, u32[]{:S(2)}) collective-permute-start(bf16[2,256,256]{2,1,0:T(8,128)(2,1)} %pad_maximum_fusion), channel_id=1, source_target_pairs={{0,4},{4,8},{8,12},{12,16},{16,20},{20,24},{24,28},{1,5},{5,9},{9,... | collective-permute-start | bytes 786440 | tf_op jit(solution)/shard_map/ppermute | solution.py:12
  11.4 7.0 %collective-permute-done.1 = bf16[2,256,256]{2,1,0:T(8,128)(2,1)S(1)} collective-permute-done((bf16[2,256,256]{2,1,0:T(8,128)(2,1)}, bf16[2,256,256]{2,1,0:T(8,128)(2,1)S(1)}, u32[]{:S(2)}, u32[]{:S(2)}) %collective-permute-start.1) | collective-permute-done | bytes 262176 | tf_op jit(solution)/shard_map/ppermute | solution.py:12
  18.4 1.0 maximum_maximum_fusion.1
  19.5 3.2 %collective-permute-start.2 = (bf16[2,512,256]{2,1,0:T(8,128)(2,1)S(1)}, bf16[2,512,256]{2,1,0:T(8,128)(2,1)}, u32[]{:S(2)}, u32[]{:S(2)}) collective-permute-start(bf16[2,512,256]{2,1,0:T(8,128)(2,1)S(1)} %maximum_maximum_fusion.1), channel_id=1, source_target_pairs={{0,8},{4,12},{8,16},{12,20},{16,24},{20,28},{1,9},{5,13},{9,17},{1... | collective-permute-start | bytes 1572872 | tf_op jit(solution)/shard_map/ppermute | solution.py:12
  22.7 1.3 %collective-permute-start = (bf16[2,256,256]{2,1,0:T(8,128)(2,1)}, bf16[2,256,256]{2,1,0:T(8,128)(2,1)S(1)}, u32[]{:S(2)}, u32[]{:S(2)}) collective-permute-start(bf16[2,256,256]{2,1,0:T(8,128)(2,1)} %pad_maximum_fusion), channel_id=1, source_target_pairs={{0,16},{4,20},{8,24},{12,28},{1,17},{5,21},{9,25},{13,29},{2,18},{... | collective-permute-start | bytes 786440 | tf_op jit(solution)/shard_map/ppermute | solution.py:12
  24.0 0.8 reduce-window.8
  24.8 1.2 %copy.17 = bf16[256,1024]{0,1:T(8,128)(2,1)S(1)} copy(bf16[256,1024]{1,0:T(8,128)(2,1)} %param.7) | data formatting | bytes 1048576 | tf_op args[0]
  26.1 0.3 copy.19
  26.4 0.1 convert_reduce_fusion.1
  26.5 12.3 %collective-permute-done = bf16[2,256,256]{2,1,0:T(8,128)(2,1)S(1)} collective-permute-done((bf16[2,256,256]{2,1,0:T(8,128)(2,1)}, bf16[2,256,256]{2,1,0:T(8,128)(2,1)S(1)}, u32[]{:S(2)}, u32[]{:S(2)}) %collective-permute-start) | collective-permute-done | bytes 262176 | tf_op jit(solution)/shard_map/ppermute | solution.py:12
  38.8 0.0 copy-start.2
  38.8 0.7 copy-done.2
  39.5 0.0 collective-permute-done.2
  39.5 0.0 copy-done
  39.5 0.0 copy-done.1
  39.5 1.2 %maximum_maximum_fusion = bf16[2,1280,256]{2,1,0:T(8,128)(2,1)S(1)} fusion(bf16[1,256,256]{2,1,0:T(8,128)(2,1)S(1)} %bitcast.63, bf16[1,256,256]{2,1,0:T(8,128)(2,1)S(1)} %bitcast.66, bf16[2,256,256]{2,1,0:T(8,128)(2,1)S(1)} %collective-permute-done.1, bf16[2,512,256]{2,1,0:T(8,128)(2,1)} %collective-permute-done.2, bf16[2,256,256]{2,1,0:T(8,128)(2,1)} %copy-done.2), kind=kLoop, calls=%fused_computation.28 | loop fusion | flops 6553600 | bytes 2621440 | tf_op jit(solution)/shard_map/concatenate | solution.py:32
  40.7 14.0 %while.15 = (s32[]{:T(128)}, f32[2,4,256]{2,1,0:T(4,128)S(1)}, f32[2,4,256]{2,1,0:T(4,128)S(1)}, f32[2,4,256,128]{3,2,1,0:T(8,128)S(1)}, s32[5,256]{1,0:T(8,128)...) while((s32[]{:T(128)}, f32[2,4,256]{2,1,0:T(4,128)S(1)}, ...), condition=%wide.region_6.7_spmd.clone, body=%wide.region_2.6_spmd.clone.sunk | while | flops 276316416 | bytes 10626765 | solution.py:77
  40.7 0.1 convert_reduce_fusion.3
  40.8 0.2 and_and_fusion.2
  41.0 0.1 copy.33
  41.1 0.1 copy.34
  41.2 0.5 fusion.31
  41.8 0.5 fusion.32
  42.4 1.1 %convolution_add_fusion.2 = f32[2,4,256,128]{3,2,1,0:T(8,128)S(1)} fusion(bf16[256,2,128,1]{0,2,3,1:T(8,128)(2,1)S(1)} %bitcast.58, f32[2,256,256,4]{2,1,3,0:T(8,128)S(1)} %get-tuple-element.217, f32[2,4,256,128]{3,2,1,0:T(8,128)S(1)} %get-tuple-element.237, f32[2,4,256]{2,1,0:T(4,128)S(1)} %select_maximum_fusion.2, ...), kind=kOutput, calls=%fused_computation.6.clone.1 | convolution fusion | flops 137625600 | bytes 4407297 | tf_op jit(solution)/shard_map/while/body/eval_jaxpr/wcju,uwn->wcjn/dot_general | solution.py:63
  43.5 0.1 convert_reduce_fusion.3
  43.6 0.2 and_and_fusion.2
  43.8 0.1 copy.33
  43.9 0.1 copy.34
  44.0 0.5 fusion.31
  44.6 0.5 fusion.32
  45.2 1.1 %convolution_add_fusion.2 = f32[2,4,256,128]{3,2,1,0:T(8,128)S(1)} fusion(bf16[256,2,128,1]{0,2,3,1:T(8,128)(2,1)S(1)} %bitcast.58, f32[2,256,256,4]{2,1,3,0:T(8,128)S(1)} %get-tuple-element.217, f32[2,4,256,128]{3,2,1,0:T(8,128)S(1)} %get-tuple-element.237, f32[2,4,256]{2,1,0:T(4,128)S(1)} %select_maximum_fusion.2, ...), kind=kOutput, calls=%fused_computation.6.clone.1 | convolution fusion | flops 137625600 | bytes 4407297 | tf_op jit(solution)/shard_map/while/body/eval_jaxpr/wcju,uwn->wcjn/dot_general | solution.py:63
  46.3 0.1 convert_reduce_fusion.3
  46.4 0.2 and_and_fusion.2
  46.6 0.1 copy.33
  46.7 0.1 copy.34
  46.9 0.5 fusion.31
  47.4 0.5 fusion.32
  48.0 1.1 %convolution_add_fusion.2 = f32[2,4,256,128]{3,2,1,0:T(8,128)S(1)} fusion(bf16[256,2,128,1]{0,2,3,1:T(8,128)(2,1)S(1)} %bitcast.58, f32[2,256,256,4]{2,1,3,0:T(8,128)S(1)} %get-tuple-element.217, f32[2,4,256,128]{3,2,1,0:T(8,128)S(1)} %get-tuple-element.237, f32[2,4,256]{2,1,0:T(4,128)S(1)} %select_maximum_fusion.2, ...), kind=kOutput, calls=%fused_computation.6.clone.1 | convolution fusion | flops 137625600 | bytes 4407297 | tf_op jit(solution)/shard_map/while/body/eval_jaxpr/wcju,uwn->wcjn/dot_general | solution.py:63
  49.1 0.1 convert_reduce_fusion.3
  49.2 0.2 and_and_fusion.2
  49.4 0.1 copy.33
  49.5 0.1 copy.34
  49.6 0.5 fusion.31
  50.2 0.5 fusion.32
  50.8 1.1 %convolution_add_fusion.2 = f32[2,4,256,128]{3,2,1,0:T(8,128)S(1)} fusion(bf16[256,2,128,1]{0,2,3,1:T(8,128)(2,1)S(1)} %bitcast.58, f32[2,256,256,4]{2,1,3,0:T(8,128)S(1)} %get-tuple-element.217, f32[2,4,256,128]{3,2,1,0:T(8,128)S(1)} %get-tuple-element.237, f32[2,4,256]{2,1,0:T(4,128)S(1)} %select_maximum_fusion.2, ...), kind=kOutput, calls=%fused_computation.6.clone.1 | convolution fusion | flops 137625600 | bytes 4407297 | tf_op jit(solution)/shard_map/while/body/eval_jaxpr/wcju,uwn->wcjn/dot_general | solution.py:63
  51.9 0.1 convert_reduce_fusion.3
  52.0 0.2 and_and_fusion.2
  52.2 0.1 copy.33
  52.3 0.1 copy.34
  52.5 0.5 fusion.31
  53.0 0.5 fusion.32
  53.6 1.1 %convolution_add_fusion.2 = f32[2,4,256,128]{3,2,1,0:T(8,128)S(1)} fusion(bf16[256,2,128,1]{0,2,3,1:T(8,128)(2,1)S(1)} %bitcast.58, f32[2,256,256,4]{2,1,3,0:T(8,128)S(1)} %get-tuple-element.217, f32[2,4,256,128]{3,2,1,0:T(8,128)S(1)} %get-tuple-element.237, f32[2,4,256]{2,1,0:T(4,128)S(1)} %select_maximum_fusion.2, ...), kind=kOutput, calls=%fused_computation.6.clone.1 | convolution fusion | flops 137625600 | bytes 4407297 | tf_op jit(solution)/shard_map/while/body/eval_jaxpr/wcju,uwn->wcjn/dot_general | solution.py:63
  54.7 0.3 copy.20
  55.0 0.1 divide_convert_fusion
  55.1 7.1 %convolution_convert_fusion = bf16[256,4096]{1,0:T(8,128)(2,1)} fusion(bf16[256,1024]{0,1:T(8,128)(2,1)S(1)} %bitcast.59, bf16[1024,4096]{1,0:T(8,128)(2,1)} %param.11), kind=kOutput, calls=%fused_computation.27 | convolution fusion | flops 2148532224 | bytes 11010048 | tf_op jit(solution)/shard_map/dot_general | solution.py:85
  62.3 0.0 reduce-scatter.2.cloned.1.call-update
  62.3 39.1 %reduce-scatter.2.cloned.1.call-done = bf16[64,4096]{1,0:T(8,128)(2,1)} async-done(((bf16[256,4096]{1,0:T(8,128)(2,1)}), bf16[64,4096]{1,0:T(8,128)(2,1)}) %reduce-scatter.2.cloned.1.call-update) | async-done | bytes 524304 | tf_op jit(solution)/shard_map/reduce_scatter | solution.py:84
  (35 shorter events, 0.5 us)
Async XLA Ops:
  6.5 32.9 %copy-start = (bf16[256,256]{1,0:T(8,128)(2,1)S(1)}, bf16[256,256]{1,0:T(8,128)(2,1)}, u32[]{:S(2)}) copy-start(bf16[256,256]{1,0:T(8,128)(2,1)} %param.9) | copy-start | bytes 393220
  6.5 32.9 %copy-start.1 = (bf16[256,256]{1,0:T(8,128)(2,1)S(1)}, bf16[256,256]{1,0:T(8,128)(2,1)}, u32[]{:S(2)}) copy-start(bf16[256,256]{1,0:T(8,128)(2,1)} %param.8) | copy-start | bytes 393220
  6.5 94.9 %reduce-scatter.2.cloned.1.call-start = ((), (), s32[]{:S(2)}) async-start(), calls=%async_computation.1 | async-start | bytes 2621440 | tf_op jit(solution)/shard_map/reduce_scatter | solution.py:84
  8.3 10.2 %collective-permute-start.1 = (bf16[2,256,256]{2,1,0:T(8,128)(2,1)}, bf16[2,256,256]{2,1,0:T(8,128)(2,1)S(1)}, u32[]{:S(2)}, u32[]{:S(2)}) collective-permute-start(bf16[2,256,256]{2,1,0:T(8,128)(2,1)} %pad_maximum_fusion), channel_id=1, source_target_pairs={{0,4},{4,8},{8,12},{12,16},{16,20},{20,24},{24,28},{1,5},{5,9},{9,... | collective-permute-start | bytes 786440 | tf_op jit(solution)/shard_map/ppermute | solution.py:12
  19.5 20.0 %collective-permute-start.2 = (bf16[2,512,256]{2,1,0:T(8,128)(2,1)S(1)}, bf16[2,512,256]{2,1,0:T(8,128)(2,1)}, u32[]{:S(2)}, u32[]{:S(2)}) collective-permute-start(bf16[2,512,256]{2,1,0:T(8,128)(2,1)S(1)} %maximum_maximum_fusion.1), channel_id=1, source_target_pairs={{0,8},{4,12},{8,16},{12,20},{16,24},{20,28},{1,9},{5,13},{9,17},{1... | collective-permute-start | bytes 1572872 | tf_op jit(solution)/shard_map/ppermute | solution.py:12
  22.7 16.1 %collective-permute-start = (bf16[2,256,256]{2,1,0:T(8,128)(2,1)}, bf16[2,256,256]{2,1,0:T(8,128)(2,1)S(1)}, u32[]{:S(2)}, u32[]{:S(2)}) collective-permute-start(bf16[2,256,256]{2,1,0:T(8,128)(2,1)} %pad_maximum_fusion), channel_id=1, source_target_pairs={{0,16},{4,20},{8,24},{12,28},{1,17},{5,21},{9,25},{13,29},{2,18},{... | collective-permute-start | bytes 786440 | tf_op jit(solution)/shard_map/ppermute | solution.py:12
  38.8 0.7 copy-start.2
Sparse Core Ops, SparseCore 0:
  62.4 38.9 reduce-scatter.1
where the time goes:
time: 110 us; the launch traced here: 108 us
  waiting for transfers between devices  58.5 us (53%)
  matrix products  15.4 us (14%)
  between operations  13.5 us (12%)
  other arithmetic  9.16 us (8%)
  starting transfers between devices  7.61 us (7%)
  local copies, waits for them, and re-layouts  3.7 us (3%)
    reduce_scatter x1, waiting for transfers between devices, shards(): lax.psum_scatter(jnp.dot(attended, out_weight, preferred_element_type=jnp...  39.1 us
    ppermute x3, waiting for transfers between devices, shifted(): lax.ppermute(value, axis, [(source, source + steps) for source in range(f...  19.3 us
    ppermute x3, starting transfers between devices, shifted(): lax.ppermute(value, axis, [(source, source + steps) for source in range(f...  7.6 us
    dot_general x1, matrix products, shards(): jnp.dot(attended, out_weight, preferred_element_type=jnp.float32)  7.12 us
    dot_general x5, matrix products, step(): jnp.einsum('wcju,uwn->wcjn', weights.astype(jnp.bfloat16), value_heads, p...  5.5 us
    dot_general x5, matrix products, step(): jnp.einsum('hqnp,zqp->qnhz', query_head_rows, key_head_rows, preferred_el...  2.73 us
    reduce_sum x5, other arithmetic, step(): total = total * factor + jnp.sum(weights, axis=-1)  2.63 us
    unnamed x8, local copies, waits for them, and re-layouts  2.22 us
  transfers between devices with their start and end apart: 4, of which 3 were waited for; matrix products, arithmetic and copies ran while one was open for 2% of the time, Pallas kernels for 0%

commit v1 on v0

--- a/solution.py
+++ b/solution.py
@@ -1,9 +1,295 @@
+import math
+
 import jax
 import jax.numpy as jnp
 from jax import lax
+from jax.experimental import pallas as pl
+from jax.experimental.pallas import tpu as pltpu
 from jax.sharding import PartitionSpec as P
 
 HEAD_SIZE = 128
+MESH = pl.DeviceIdType.MESH
+MASKED = -1.2e31
+CHUNK = 512
+
+
+def fused_kernel(
+    lengths, queries, keys, values, weight, out,
+    q_vm, kv_own, window, w_vm, q_t, top, total, accum, att,
+    near_send, near_recv, far_send, far_recv, pair_send, pair_recv, far_keep, own_keep,
+    load_sem, w_sem, up_send, up_recv, side_send, side_recv, core_send, core_recv, y_send, y_recv,
+):
+    tok = q_vm.shape[0]
+    local_kv = kv_own.shape[1]
+    heads = q_t.shape[0]
+    group = heads // local_kv
+    chunks = w_vm.shape[0]
+    rows = tok // 4
+    scale = math.log2(math.e) / math.sqrt(HEAD_SIZE)
+
+    ctx = lax.axis_index("ctx")
+    head = lax.axis_index("head")
+    z, x = ctx // 2, ctx % 2
+    y, core = head // 2, head % 2
+    last = lax.axis_size("ctx") // 2 - 1
+    side = 2 * z + 1 - x
+    core_nbr = 2 * y + 1 - core
+    y_nbr = 2 * (1 - y) + core
+
+    loads = [pltpu.make_async_copy(queries, q_vm, load_sem.at[0])]
+    for h in range(local_kv):
+        lanes = pl.ds(h * HEAD_SIZE, HEAD_SIZE)
+        loads.append(pltpu.make_async_copy(keys.at[:, lanes], kv_own.at[0, h], load_sem.at[1 + 2 * h]))
+        loads.append(pltpu.make_async_copy(values.at[:, lanes], kv_own.at[1, h], load_sem.at[2 + 2 * h]))
+    for load in loads:
+        load.start()
+
+    barrier = pltpu.get_barrier_semaphore()
+
+    def greet(c, h):
+        pl.semaphore_signal(barrier, inc=1, device_id=(c, h), device_id_type=MESH)
+
+    greet(side, head)
+    greet(ctx, core_nbr)
+    greet(ctx, y_nbr)
+
+    @pl.when(z > 0)
+    def _():
+        greet(ctx - 2, head)
+
+    @pl.when(z < last)
+    def _():
+        greet(ctx + 2, head)
+
+    pl.semaphore_wait(barrier, 3 + jnp.minimum(z, 1) + jnp.minimum(last - z, 1))
+
+    def remote(src, dst, send, recv, c, h):
+        return pltpu.make_async_remote_copy(
+            src_ref=src, dst_ref=dst, send_sem=send, recv_sem=recv, device_id=(c, h), device_id_type=MESH
+        )
+
+    def own(t, h):
+        source = keys if t == 0 else values
+        return source.at[:, pl.ds(h * HEAD_SIZE, HEAD_SIZE)]
+
+    def up(which, t, h):
+        src = own(t, h) if which == 0 else window.at[1, t, h]
+        return remote(src, window.at[1 + 2 * which, t, h], up_send.at[which, t, h], up_recv.at[which, t, h], ctx + 2, head)
+
+    def side_from(src, which, t, h):
+        return remote(src, window.at[2 * which, t, h], side_send.at[which, t, h], side_recv.at[which, t, h], side, head)
+
+    for h in range(local_kv):
+        for t in range(2):
+            @pl.when(z < last)
+            def _():
+                up(0, t, h).start()
+
+            @pl.when(x == 0)
+            def _():
+                side_from(own(t, h), 0, t, h).start()
+
+    w_loads = [
+        pltpu.make_async_copy(weight.at[:, pl.ds(c * CHUNK, CHUNK)], w_vm.at[c], w_sem.at[c]) for c in range(chunks)
+    ]
+    for load in w_loads:
+        load.start()
+
+    query_pos = ctx * tok + lax.broadcasted_iota(jnp.int32, (1, tok), 1)
+    begin = jnp.zeros((1, tok), jnp.int32)
+    end = jnp.int32(0)
+    for n in range(lengths.shape[0]):
+        end = end + lengths[n]
+        begin = jnp.where(query_pos >= end, end, begin)
+    key_row = lax.broadcasted_iota(jnp.int32, (tok, tok), 0)
+
+    for load in loads:
+        load.wait()
+    for n in range(heads):
+        q_t[n] = q_vm[:, n * HEAD_SIZE : (n + 1) * HEAD_SIZE].T
+
+    def attend(h, distance):
+        ref = kv_own if distance == 0 else window.at[distance - 1]
+        key = ref[0, h]
+        value_t = ref[1, h].T
+        key_pos = key_row + (ctx - distance) * tok
+        allowed = key_pos >= begin
+        if distance == 0:
+            allowed = allowed & (key_pos <= query_pos)
+        for j in range(group):
+            n = h * group + j
+            s = jnp.dot(key, q_t[n], preferred_element_type=jnp.float32)
+            s = jnp.where(allowed, s, jnp.float32(MASKED))
+            newest = jnp.max(s, axis=0, keepdims=True)
+            if distance:
+                before = top[n]
+                newest = jnp.maximum(before, newest)
+                factor = jnp.exp2((before - newest) * scale)
+            weights = jnp.exp2((s - newest) * scale)
+            added = jnp.sum(weights, axis=0, keepdims=True)
+            product = jnp.dot(value_t, weights.astype(jnp.bfloat16), preferred_element_type=jnp.float32)
+            if distance:
+                added = total[n] * factor + added
+                product = accum[n] * factor + product
+            top[n] = newest
+            total[n] = added
+            accum[n] = product
+
+    def attend_if(h, distance):
+        @pl.when(ctx >= distance)
+        def _():
+            attend(h, distance)
+
+    def relay(which, h):
+        @pl.when(z > which)
+        def _():
+            for t in range(2):
+                up(which, t, h).wait_recv()
+                if which == 0:
+                    @pl.when(z < last)
+                    def _():
+                        up(1, t, h).start()
+
+                    @pl.when(x == 0)
+                    def _():
+                        side_from(window.at[1, t, h], 1, t, h).start()
+
+                    @pl.when(x == 1)
+                    def _():
+                        side_from(window.at[1, t, h], 0, t, h).start()
+                else:
+                    @pl.when(x == 1)
+                    def _():
+                        side_from(window.at[3, t, h], 1, t, h).start()
+
+    def side_arrived(which, h):
+        @pl.when(ctx >= 1 + 2 * which)
+        def _():
+            for t in range(2):
+                side_from(own(t, h), which, t, h).wait_recv()
+
+    attend(0, 0)
+    relay(0, 0)
+    attend(1, 0)
+    attend_if(0, 2)
+    relay(0, 1)
+    attend_if(1, 2)
+    side_arrived(0, 0)
+    attend_if(0, 1)
+    relay(1, 0)
+    side_arrived(0, 1)
+    attend_if(1, 1)
+    attend_if(0, 4)
+    relay(1, 1)
+    attend_if(1, 4)
+    side_arrived(1, 0)
+    attend_if(0, 3)
+    side_arrived(1, 1)
+    attend_if(1, 3)
+
+    for n in range(heads):
+        ready = (accum[n] / total[n]).T.astype(jnp.bfloat16)
+        for g in range(4):
+            place = ((g // 2 + y) % 2) * 2 + (g % 2 + core) % 2
+            att[pl.ds(pl.multiple_of(place * rows, rows), rows), n * HEAD_SIZE : (n + 1) * HEAD_SIZE] = ready[
+                g * rows : (g + 1) * rows
+            ]
+
+    def far(c):
+        return remote(far_send.at[c], far_recv.at[c], core_send.at[0, c], core_recv.at[0, c], ctx, core_nbr)
+
+    def near(c):
+        return remote(near_send.at[c], near_recv.at[c], core_send.at[1, c], core_recv.at[1, c], ctx, core_nbr)
+
+    def across(c):
+        return remote(pair_send.at[c], pair_recv.at[c], y_send.at[c], y_recv.at[c], ctx, y_nbr)
+
+    def project(c):
+        w_loads[c].wait()
+        partial = jnp.dot(att[...], w_vm[c], preferred_element_type=jnp.float32)
+        far_send[c] = partial[3 * rows :].astype(jnp.bfloat16)
+        far(c).start()
+        far_keep[c] = partial[2 * rows : 3 * rows]
+        near_send[c] = partial[rows : 2 * rows].astype(jnp.bfloat16)
+        near(c).start()
+        own_keep[c] = partial[:rows]
+
+    def pass_on(c):
+        far(c).wait_recv()
+        pair_send[c] = (far_keep[c] + far_recv[c].astype(jnp.float32)).astype(jnp.bfloat16)
+        across(c).start()
+
+    for c in range(chunks):
+        project(c)
+        if c:
+            pass_on(c - 1)
+    pass_on(chunks - 1)
+    for c in range(chunks):
+        near(c).wait_recv()
+        across(c).wait_recv()
+        out[:, c * CHUNK : (c + 1) * CHUNK] = (
+            own_keep[c] + near_recv[c].astype(jnp.float32) + pair_recv[c].astype(jnp.float32)
+        ).astype(jnp.bfloat16)
+
+    for h in range(local_kv):
+        for t in range(2):
+            @pl.when(z < last)
+            def _():
+                up(0, t, h).wait_send()
+
+            @pl.when((z < last) & (z > 0))
+            def _():
+                up(1, t, h).wait_send()
+
+            @pl.when((x == 0) | (z > 0))
+            def _():
+                side_from(own(t, h), 0, t, h).wait_send()
+
+            @pl.when(z > x)
+            def _():
+                side_from(own(t, h), 1, t, h).wait_send()
+    for c in range(chunks):
+        far(c).wait_send()
+        near(c).wait_send()
+        across(c).wait_send()
+
+
+def fused_shards(queries, keys, values, lengths, out_weight):
+    tok = queries.shape[0]
+    local_kv = keys.shape[1] // HEAD_SIZE
+    heads = queries.shape[1] // HEAD_SIZE
+    columns = out_weight.shape[1]
+    chunks = columns // CHUNK
+    rows = tok // 4
+    piece = (chunks, rows, CHUNK)
+    bf16, f32 = jnp.bfloat16, jnp.float32
+    dma = pltpu.SemaphoreType.DMA
+    return pl.pallas_call(
+        fused_kernel,
+        out_shape=jax.ShapeDtypeStruct((rows, columns), bf16),
+        in_specs=[pl.BlockSpec(memory_space=pltpu.SMEM)] + [pl.BlockSpec(memory_space=pl.ANY)] * 4,
+        out_specs=pl.BlockSpec(memory_space=pltpu.VMEM),
+        scratch_shapes=[
+            pltpu.VMEM(queries.shape, bf16),
+            pltpu.VMEM((2, local_kv, tok, HEAD_SIZE), bf16),
+            pltpu.VMEM((4, 2, local_kv, tok, HEAD_SIZE), bf16),
+            pltpu.VMEM((chunks, out_weight.shape[0], CHUNK), bf16),
+            pltpu.VMEM((heads, HEAD_SIZE, tok), bf16),
+            pltpu.VMEM((heads, 1, tok), f32),
+            pltpu.VMEM((heads, 1, tok), f32),
+            pltpu.VMEM((heads, HEAD_SIZE, tok), f32),
+            pltpu.VMEM((tok, heads * HEAD_SIZE), bf16),
+        ]
+        + [pltpu.VMEM(piece, bf16)] * 6
+        + [pltpu.VMEM(piece, f32)] * 2
+        + [dma((1 + 2 * local_kv,)), dma((chunks,))]
+        + [dma((2, 2, local_kv))] * 4
+        + [dma((2, chunks))] * 2
+        + [dma((chunks,))] * 2,
+        compiler_params=pltpu.CompilerParams(
+            collective_id=0, has_side_effects=True, vmem_limit_bytes=60 * 1024 * 1024
+        ),
+    )(lengths, queries, keys, values, out_weight)
 
 
 def shifted(value, axis, steps):
@@ -22,7 +308,8 @@
     query_group = queries.shape[1] // keys.shape[1]
     span = min(16, lax.axis_size("ctx") // 2)
     stretch = lax.axis_index("ctx")
-    ends = jnp.cumsum(lengths)
+    order = jnp.arange(lengths.shape[0])
+    ends = jnp.sum(jnp.where(order[None, :] <= order[:, None], lengths[None, :], 0), axis=1)
     paired = jnp.stack([keys, values])
     window = paired
     have = 1
@@ -92,4 +379,5 @@
 def solution(mesh):
     in_specs = (P("ctx", "head"), P("ctx", "head"), P("ctx", "head"), P(), P("head", None))
     out_specs = P(("ctx", "head"), None)
-    return jax.shard_map(shards, mesh=mesh, in_specs=in_specs, out_specs=out_specs, check_vma=False)
+    body = fused_shards if (mesh.shape["ctx"], mesh.shape["head"]) == (8, 4) else shards
+    return jax.shard_map(body, mesh=mesh, in_specs=in_specs, out_specs=out_specs, check_vma=False)

time: 110 us -> 41.2 us (0.37); the launches traced: 108 us -> 41 us
  waiting for transfers between devices: 58.5 us -> 0 us
  Pallas kernels: 0 us -> 39.2 us
  matrix products: 15.4 us -> 0 us
  between operations: 13.5 us -> 0.01 us
  other arithmetic: 9.16 us -> 0 us
  starting transfers between devices: 7.61 us -> 0 us
  local copies, waits for them, and re-layouts: 3.7 us -> 1.87 us
    pallas_call x0 -> x1, Pallas kernels: none -> 39.2 us  [fused_shards(): pl.pallas_call(fused_kernel, out_shape=jax.ShapeDtypeStruct((rows, column...]
    reduce_scatter x1 -> x0, waiting for transfers between devices: 39.1 us -> none  [shards(): lax.psum_scatter(jnp.dot(attended, out_weight, preferred_element_type=jnp...]
    ppermute x3 -> x0, waiting for transfers between devices: 19.3 us -> none  [shifted(): lax.ppermute(value, axis, [(source, source + steps) for source in range(f...]
    dot_general x11 -> x0, matrix products: 15.4 us -> none  [the longest x1 7.12 us: shards(): jnp.dot(attended, out_weight, preferred_element_type=jnp.float32)]
    ppermute x3 -> x0, starting transfers between devices: 7.6 us -> none  [shifted(): lax.ppermute(value, axis, [(source, source + steps) for source in range(f...]
    reduce_sum x11 -> x0, other arithmetic: 3.13 us -> none  [the longest x5 2.63 us: step(): total = total * factor + jnp.sum(weights, axis=-1)]
    another operation x2 -> x0, other arithmetic: 2.57 us -> none  [the longest x1 1.74 us: shards(): paired = jnp.stack([keys, values])]
    concatenate x2 -> x0, other arithmetic: 2.2 us -> none  [shards(): window = jnp.concatenate([received, window], axis=1)]
  transfers between devices with their start and end apart: 4 -> 0, of which waited for: 3 -> 0; matrix products, arithmetic and copies ran while one was open for 2% -> 0% of each run, Pallas kernels for 0% -> 0%
where the time goes in v1:
time: 41.2 us; the launch traced here: 41 us
  Pallas kernels  39.2 us (95%)
  local copies, waits for them, and re-layouts  1.87 us (5%)
    pallas_call x1, Pallas kernels, fused_shards(): pl.pallas_call(fused_kernel, out_shape=jax.ShapeDtypeStruct((rows, column...  39.2 us
    unnamed x1, local copies, waits for them, and re-layouts  1.87 us

profile of v1, /device:TPU:17, one launch (start us, length us, event | category | flops | bytes accessed | tf_op | source)
XLA Modules:
  0.0 41.0 jit_solution(10512625194164340443)
XLA Ops:
  0.0 39.2 %shard_map.55 = bf16[64,4096]{1,0:T(8,128)(2,1)} custom-call(s32[8]{0:T(128)} %lengths.1, bf16[256,1024]{1,0:T(8,128)(2,1)} %queries.1, bf16[256,256]{1,0:T(8,128)(2,1)} %keys.1, bf16[256,256]{1,0:T(8,128)(2,1)} %values.1, bf16[1024,4096]{1,0:T(8,128)(2,1)} %weight.1), custom_call_target="tpu_custom_call" | custom-call | tf_op jit(solution)/shard_map/pallas_call | solution.py:267
  39.2 1.9 %copy.7 = bf16[64,4096]{1,0:T(8,128)(2,1)} copy(bf16[64,4096]{1,0:T(8,128)(2,1)} %shard_map.55) | data formatting | bytes 1048576

commit v2 on v1

--- a/solution.py
+++ b/solution.py
@@ -116,24 +116,31 @@
         allowed = key_pos >= begin
         if distance == 0:
             allowed = allowed & (key_pos <= query_pos)
-        for j in range(group):
-            n = h * group + j
-            s = jnp.dot(key, q_t[n], preferred_element_type=jnp.float32)
-            s = jnp.where(allowed, s, jnp.float32(MASKED))
+        tiles = [(h * group + j, pl.ds(i * 128, 128), i) for j in range(group) for i in range(tok // 128)]
+
+        def scores(tile):
+            return jnp.dot(key, q_t[tile[0], :, tile[1]], preferred_element_type=jnp.float32)
+
+        masks = [allowed[:, i * 128 : (i + 1) * 128] for i in range(tok // 128)]
+        queue = [scores(tile) for tile in tiles[:4]]
+        for place, (n, lanes, i) in enumerate(tiles):
+            if place + 4 < len(tiles):
+                queue.append(scores(tiles[place + 4]))
+            s = jnp.where(masks[i], queue[place], jnp.float32(MASKED))
             newest = jnp.max(s, axis=0, keepdims=True)
             if distance:
-                before = top[n]
+                before = top[n, :, lanes]
                 newest = jnp.maximum(before, newest)
                 factor = jnp.exp2((before - newest) * scale)
             weights = jnp.exp2((s - newest) * scale)
             added = jnp.sum(weights, axis=0, keepdims=True)
             product = jnp.dot(value_t, weights.astype(jnp.bfloat16), preferred_element_type=jnp.float32)
             if distance:
-                added = total[n] * factor + added
-                product = accum[n] * factor + product
-            top[n] = newest
-            total[n] = added
-            accum[n] = product
+                added = total[n, :, lanes] * factor + added
+                product = accum[n, :, lanes] * factor + product
+            top[n, :, lanes] = newest
+            total[n, :, lanes] = added
+            accum[n, :, lanes] = product
 
     def attend_if(h, distance):
         @pl.when(ctx >= distance)
@@ -167,6 +174,15 @@
         def _():
             for t in range(2):
                 side_from(own(t, h), which, t, h).wait_recv()
+
+    def finish(h):
+        for n in range(h * group, (h + 1) * group):
+            ready = (accum[n] / total[n]).T.astype(jnp.bfloat16)
+            for g in range(4):
+                place = ((g // 2 + y) % 2) * 2 + (g % 2 + core) % 2
+                att[pl.ds(pl.multiple_of(place * rows, rows), rows), n * HEAD_SIZE : (n + 1) * HEAD_SIZE] = ready[
+                    g * rows : (g + 1) * rows
+                ]
 
     attend(0, 0)
     relay(0, 0)
@@ -184,16 +200,10 @@
     attend_if(1, 4)
     side_arrived(1, 0)
     attend_if(0, 3)
+    finish(0)
     side_arrived(1, 1)
     attend_if(1, 3)
-
-    for n in range(heads):
-        ready = (accum[n] / total[n]).T.astype(jnp.bfloat16)
-        for g in range(4):
-            place = ((g // 2 + y) % 2) * 2 + (g % 2 + core) % 2
-            att[pl.ds(pl.multiple_of(place * rows, rows), rows), n * HEAD_SIZE : (n + 1) * HEAD_SIZE] = ready[
-                g * rows : (g + 1) * rows
-            ]
+    finish(1)
 
     def far(c):
         return remote(far_send.at[c], far_recv.at[c], core_send.at[0, c], core_recv.at[0, c], ctx, core_nbr)

time: 41.2 us -> 38.6 us (0.937)
  Pallas kernels: 39.2 us -> 36.6 us
    pallas_call x1, Pallas kernels: 39.2 us -> 36.6 us  [fused_shards(): pl.pallas_call(fused_kernel, out_shape=jax.ShapeDtypeStruct((rows, column...]
where the time goes in v2:
time: 38.6 us; the launch traced here: 38.5 us
  Pallas kernels  36.6 us (95%)
  local copies, waits for them, and re-layouts  1.87 us (5%)
    pallas_call x1, Pallas kernels, fused_shards(): pl.pallas_call(fused_kernel, out_shape=jax.ShapeDtypeStruct((rows, column...  36.6 us
    unnamed x1, local copies, waits for them, and re-layouts  1.87 us

profile of v2, /device:TPU:17, one launch (start us, length us, event | category | flops | bytes accessed | tf_op | source)
XLA Modules:
  0.0 38.5 jit_solution(1815125504861279291)
XLA Ops:
  0.0 36.6 %shard_map.55 = bf16[64,4096]{1,0:T(8,128)(2,1)} custom-call(s32[8]{0:T(128)} %lengths.1, bf16[256,1024]{1,0:T(8,128)(2,1)} %queries.1, bf16[256,256]{1,0:T(8,128)(2,1)} %keys.1, bf16[256,256]{1,0:T(8,128)(2,1)} %values.1, bf16[1024,4096]{1,0:T(8,128)(2,1)} %weight.1), custom_call_target="tpu_custom_call" | custom-call | tf_op jit(solution)/shard_map/pallas_call | solution.py:277
  36.6 1.9 %copy.7 = bf16[64,4096]{1,0:T(8,128)(2,1)} copy(bf16[64,4096]{1,0:T(8,128)(2,1)} %shard_map.55) | data formatting | bytes 1048576

commit v3 on v2

--- a/solution.py
+++ b/solution.py
@@ -14,10 +14,10 @@
 
 
 def fused_kernel(
-    lengths, queries, keys, values, weight, out,
+    lengths, queries, keys, values, weight, mine, theirs,
     q_vm, kv_own, window, w_vm, q_t, top, total, accum, att,
-    near_send, near_recv, far_send, far_recv, pair_send, pair_recv, far_keep, own_keep,
-    load_sem, w_sem, up_send, up_recv, side_send, side_recv, core_send, core_recv, y_send, y_recv,
+    near_send, near_recv, far_send, far_recv, pair_send, far_keep, own_keep,
+    load_sem, w_sem, up_send, up_recv, side_send, side_recv, core_send, core_recv, y_send, y_recv, mine_sem,
 ):
     tok = q_vm.shape[0]
     local_kv = kv_own.shape[1]
@@ -212,7 +212,7 @@
         return remote(near_send.at[c], near_recv.at[c], core_send.at[1, c], core_recv.at[1, c], ctx, core_nbr)
 
     def across(c):
-        return remote(pair_send.at[c], pair_recv.at[c], y_send.at[c], y_recv.at[c], ctx, y_nbr)
+        return remote(pair_send.at[c], theirs.at[:, pl.ds(c * CHUNK, CHUNK)], y_send.at[c], y_recv.at[c], ctx, y_nbr)
 
     def project(c):
         w_loads[c].wait()
@@ -234,12 +234,16 @@
         if c:
             pass_on(c - 1)
     pass_on(chunks - 1)
+    stores = [
+        pltpu.make_async_copy(own_keep.at[c], mine.at[:, pl.ds(c * CHUNK, CHUNK)], mine_sem.at[c]) for c in range(chunks)
+    ]
     for c in range(chunks):
         near(c).wait_recv()
+        own_keep[c] += near_recv[c].astype(jnp.float32)
+        stores[c].start()
+    for c in range(chunks):
+        stores[c].wait()
         across(c).wait_recv()
-        out[:, c * CHUNK : (c + 1) * CHUNK] = (
-            own_keep[c] + near_recv[c].astype(jnp.float32) + pair_recv[c].astype(jnp.float32)
-        ).astype(jnp.bfloat16)
 
     for h in range(local_kv):
         for t in range(2):
@@ -274,11 +278,11 @@
     piece = (chunks, rows, CHUNK)
     bf16, f32 = jnp.bfloat16, jnp.float32
     dma = pltpu.SemaphoreType.DMA
-    return pl.pallas_call(
+    mine, theirs = pl.pallas_call(
         fused_kernel,
-        out_shape=jax.ShapeDtypeStruct((rows, columns), bf16),
+        out_shape=[jax.ShapeDtypeStruct((rows, columns), f32), jax.ShapeDtypeStruct((rows, columns), bf16)],
         in_specs=[pl.BlockSpec(memory_space=pltpu.SMEM)] + [pl.BlockSpec(memory_space=pl.ANY)] * 4,
-        out_specs=pl.BlockSpec(memory_space=pltpu.VMEM),
+        out_specs=[pl.BlockSpec(memory_space=pl.ANY)] * 2,
         scratch_shapes=[
             pltpu.VMEM(queries.shape, bf16),
             pltpu.VMEM((2, local_kv, tok, HEAD_SIZE), bf16),
@@ -290,16 +294,17 @@
             pltpu.VMEM((heads, HEAD_SIZE, tok), f32),
             pltpu.VMEM((tok, heads * HEAD_SIZE), bf16),
         ]
-        + [pltpu.VMEM(piece, bf16)] * 6
+        + [pltpu.VMEM(piece, bf16)] * 5
         + [pltpu.VMEM(piece, f32)] * 2
         + [dma((1 + 2 * local_kv,)), dma((chunks,))]
         + [dma((2, 2, local_kv))] * 4
         + [dma((2, chunks))] * 2
-        + [dma((chunks,))] * 2,
+        + [dma((chunks,))] * 3,
         compiler_params=pltpu.CompilerParams(
             collective_id=0, has_side_effects=True, vmem_limit_bytes=60 * 1024 * 1024
         ),
     )(lengths, queries, keys, values, out_weight)
+    return (mine + theirs.astype(f32)).astype(bf16)
 
 
 def shifted(value, axis, steps):

time: 38.6 us -> 38.4 us (level)
  other arithmetic: 0 us -> 2.24 us
  local copies, waits for them, and re-layouts: 1.87 us -> 0 us
  Pallas kernels: 36.6 us -> 36 us
    convert_element_type x0 -> x1, other arithmetic: none -> 2.24 us  [fused_shards(): return (mine + theirs.astype(f32)).astype(bf16)]
    unnamed x1 -> x0, local copies, waits for them, and re-layouts: 1.87 us -> none
    pallas_call x1, Pallas kernels: 36.6 us -> 36 us  [fused_shards(): pl.pallas_call(fused_kernel, out_shape=[jax.ShapeDtypeStruct((rows, colum...]
where the time goes in v3:
time: 38.4 us; the launch traced here: 38.2 us
  Pallas kernels  36 us (94%)
  other arithmetic  2.24 us (6%)
    pallas_call x1, Pallas kernels, fused_shards(): pl.pallas_call(fused_kernel, out_shape=[jax.ShapeDtypeStruct((rows, colum...  36 us
    convert_element_type x1, other arithmetic, fused_shards(): return (mine + theirs.astype(f32)).astype(bf16)  2.24 us

profile of v3, /device:TPU:17, one launch (start us, length us, event | category | flops | bytes accessed | tf_op | source)
XLA Modules:
  0.0 38.2 jit_solution(9961985496181119687)
XLA Ops:
  0.0 36.0 %shard_map.55 = (f32[64,4096]{1,0:T(8,128)}, bf16[64,4096]{1,0:T(8,128)(2,1)}) custom-call(s32[8]{0:T(128)} %lengths.1, bf16[256,1024]{1,0:T(8,128)(2,1)} %queries.1, bf16[256,256]{1,0:T(8,128)(2,1)} %keys.1, bf16[256,256]{1,0:T(8,128)(2,1)} %values.1, bf16[1024,4096]{1,0:T(8,128)(2,1)} %weight.1), custom_call_target="tpu_custom_call" | custom-call | tf_op jit(solution)/shard_map/pallas_call | solution.py:281
  36.0 2.2 %add_convert_fusion = bf16[64,4096]{1,0:T(8,128)(2,1)} fusion(f32[64,4096]{1,0:T(8,128)} %get-tuple-element.7, bf16[64,4096]{1,0:T(8,128)(2,1)} %get-tuple-element.8), kind=kLoop, calls=%fused_computation | loop fusion | flops 786432 | bytes 2097152 | tf_op jit(solution)/shard_map/convert_element_type | solution.py:307
